TPU v7x, 256 devices: a whole 4x4x8 slice. The times are simulated.
256 devices in a mesh: layer: 16 (over y_hi, x, core), latent: 16 (over z, y_lo).
Axes of the slice: x: 4, y: 4 (y_hi: 2, y_lo: 2; y = y_hi * 2 + y_lo), z: 8, core: 2. Of those that a mesh axis runs over, the one named last changes fastest.
Arguments:
- decoder: bfloat16 [65536, 4, 2304], P(('layer', 'latent')), may hold values from -0.375 to 0.375
- code_index: int32 [4, 128, 64], replicated, may hold values from 0 to 16383, all different within a row
- code_value: bfloat16 [4, 128, 64], replicated, may hold values from 0.19921875 to 4
- bias: float32 [4, 2304], replicated, may hold values from -3 to 3
- target: bfloat16 [4, 128, 2304], replicated, may hold values from -6 to 6
Outputs:
- layer_error: float32 [4], replicated
- grad_decoder: bfloat16 [65536, 4, 2304], P(('layer', 'latent'))
- code_grad: float32 [4, 128, 64], replicated
Inputs may be any that keep to these rules, and one draw needn't show every extreme that they name: `code_index`: the 64 indices of one token in one layer are distinct.
All inputs are finite; a program needn't handle non-finite values.
Results may differ from a plain program's by a relative error of at most 0.0048.
Values may be sent and summed in bfloat16 or wider, within the bound.
A program may use at most 64 MiB of HBM per device.

v0:
```python
import functools

import jax
import jax.numpy as jnp
from jax import lax
from jax.sharding import Mesh
from jax.sharding import PartitionSpec as P

D = 2304
LAYERS = 4
TOPK = 64
TOKENS = 128
LAYER = ("layer_0", "layer_1", "layer_2")
LATENT = ("latent_0", "latent_1")
LAYER_LATENT = ("layer_0", "layer_1", "layer_2", "latent_0", "latent_1")


def by_axis(x, axes):
    return functools.reduce(lax.psum, axes, x)


def build_codes(index_rows, value_rows, offset, slab_width):
    columns = offset + lax.iota(jnp.int32, slab_width)
    matches = index_rows[:, :, None] == columns[None, None, :]
    dense = jnp.sum(jnp.where(matches, value_rows[:, :, None].astype(jnp.float32), 0.0), axis=1)
    return (matches, dense.astype(jnp.bfloat16))


def contract_rows(left, right):
    return lax.dot_general(
        left, right, (((0,), (0,)), ((), ())), preferred_element_type=jnp.float32
    )


def contract_cols(left, right):
    return lax.dot_general(
        left, right, (((1,), (1,)), ((), ())), preferred_element_type=jnp.float32
    )


def on_device(decoder, code_index, code_value, bias, target):
    layer_count = lax.axis_size(LAYER)
    latent_count = lax.axis_size(LATENT)
    group_size = layer_count // LAYERS
    slab_width = decoder.shape[0]
    layer_pos = lax.axis_index(LAYER)
    source = layer_pos // group_size
    offset = (layer_pos % group_size * latent_count + lax.axis_index(LATENT)) * slab_width
    matches, dense_codes = build_codes(
        lax.dynamic_index_in_dim(code_index, source, 0, keepdims=False),
        lax.dynamic_index_in_dim(code_value, source, 0, keepdims=False),
        offset,
        slab_width,
    )

    def forward_step(target_layer, totals):
        weight_slab = lax.dynamic_index_in_dim(decoder, target_layer, 1, keepdims=False)
        product = jnp.dot(dense_codes, weight_slab, preferred_element_type=jnp.float32)
        return lax.dynamic_update_index_in_dim(totals, product, target_layer, 0)

    partials = jnp.zeros((LAYERS, TOKENS, D), jnp.float32)
    stop_at = LAYERS
    partials = lax.fori_loop(source, stop_at, forward_step, partials)
    recon_sum = lax.psum(partials, LAYER_LATENT)
    residual = recon_sum + bias[:, None, :] - target.astype(jnp.float32)
    layer_error = jnp.mean(residual * residual, axis=(1, 2))
    error_b = residual.astype(jnp.bfloat16)

    def backward_step(target_layer, state_pair):
        grads, code_sums = state_pair
        weight_slab = lax.dynamic_index_in_dim(decoder, target_layer, 1, keepdims=False)
        target_error = lax.dynamic_index_in_dim(error_b, target_layer, 0, keepdims=False)
        grad_block = contract_rows(dense_codes, target_error).astype(jnp.bfloat16)
        grads = lax.dynamic_update_index_in_dim(grads, grad_block, target_layer, 1)
        return (grads, code_sums + contract_cols(target_error, weight_slab))

    start_pair = (
        jnp.zeros(decoder.shape, jnp.bfloat16),
        jnp.zeros((TOKENS, slab_width), jnp.float32),
    )
    grads, code_sums = lax.fori_loop(source, stop_at, backward_step, start_pair)
    picked = jnp.sum(jnp.where(matches, code_sums[:, None, :], 0.0), axis=2)
    code_parts = lax.dynamic_update_index_in_dim(
        jnp.zeros((LAYERS, TOKENS, TOPK), jnp.float32), picked, source, 0
    )
    code_grad = by_axis(code_parts, LAYER_LATENT)
    return (layer_error, grads, code_grad)


def solution(mesh):
    torus = Mesh(
        mesh.devices.reshape(2, 4, 2, 8, 2),
        ("layer_0", "layer_1", "layer_2", "latent_0", "latent_1"),
    )
    return jax.shard_map(
        on_device,
        mesh=torus,
        in_specs=(P(LAYER_LATENT, None, None), P(), P(), P(), P()),
        out_specs=(P(), P(LAYER_LATENT, None, None), P()),
        check_vma=False,
    )
```

profile of v0, /device:TPU:1, one launch (start us, length us, event | category | flops | bytes accessed | tf_op | source)
XLA Modules:
  0.0 555.3 jit_solution(16243542202462761894)
XLA Ops:
  7.3 5.0 copy.19
  13.3 2.8 fusion.17
  16.1 2.6 broadcast_in_dim.51.clone
  18.7 13.0 %while.22 = (s32[]{:T(128)}, f32[4,128,2304]{2,1,0:T(8,128)}, bf16[256,4,2304]{2,0,1:T(8,128)(2,1)}, bf16[128,256]{1,0:T(8,128)(2,1)S(1)}, s32[]{:T(128)}, /*index=5*/s32[]{:T(128)}, s32[]{:T(128)}) while((s32[]{:T(128)}, f32[4,128,2304]{2,1,0:T(8,128)}, bf16[256,4,2304]{2,0,1:T(8,128)(2,1)}, bf16[128,256]{1,0:T(8,128)(2,1)S(1)}, s32[]{:T(128)}, ...), condition=%wide.region_2.3_spmd, body=%wide.region_1.2_spmd.sunk | while | flops 150994944 | bytes 7143551 | solution.py:63
  18.7 1.8 convolution_bitcast_fusion.2
  20.8 1.1 constant_dynamic-update-slice_fusion.3
  21.9 1.8 convolution_bitcast_fusion.2
  24.1 1.1 constant_dynamic-update-slice_fusion.3
  25.2 1.8 convolution_bitcast_fusion.2
  27.3 1.1 constant_dynamic-update-slice_fusion.3
  28.4 1.8 convolution_bitcast_fusion.2
  30.6 1.1 constant_dynamic-update-slice_fusion.3
  31.8 270.1 %all-reduce.7.cloned.1.call-done = f32[4,128,2304]{2,1,0:T(8,128)} async-done(((f32[4,128,2304]{2,1,0:T(8,128)}), f32[4,128,2304]{2,1,0:T(8,128)}) %all-reduce.7.cloned.1.call-update) | async-done | bytes 4718608 | tf_op jit(solution)/shard_map/psum | solution.py:64
  301.9 4.1 fusion.19
  306.0 2.5 broadcast_in_dim.54
  308.5 13.6 %while.23 = (s32[]{:T(128)}, bf16[256,4,2304]{0,2,1:T(8,128)(2,1)}, f32[128,256]{1,0:T(8,128)S(1)}, bf16[4,128,2304]{2,1,0:T(8,128)(2,1)S(1)}, bf16[128,256]{1,0...) while((s32[]{:T(128)}, bf16[256,4,2304]{0,2,1:T(8,128)(2,1)}, ...), condition=%wide.region_6.7_spmd, body=%wide.region_5.6_spmd.sunk | while | flops 302612480 | bytes 3868807 | solution.py:81
  308.5 1.6 fusion.36
  310.1 1.8 fusion.37
  311.9 1.5 fusion.36
  313.5 1.8 fusion.37
  315.3 1.5 fusion.36
  316.8 1.8 fusion.37
  318.7 1.6 fusion.36
  320.3 1.8 fusion.37
  322.1 2.6 fusion.18
  325.6 31.9 %all-reduce.9.cloned.1.call-done = f32[4,128,64]{1,2,0:T(8,128)} async-done(((f32[4,128,64]{1,2,0:T(8,128)}), f32[4,128,64]{1,2,0:T(8,128)}) %all-reduce.9.cloned.1.call-update) | async-done | bytes 131088 | tf_op jit(solution)/shard_map/psum | solution.py:19
  357.6 46.4 %all-reduce.11.cloned.1.call-done = f32[4,128,64]{1,2,0:T(8,128)} async-done(((f32[4,128,64]{1,2,0:T(8,128)}), f32[4,128,64]{1,2,0:T(8,128)}) %all-reduce.11.cloned.1.call-update) | async-done | bytes 131088 | tf_op jit(solution)/shard_map/psum | solution.py:19
  404.1 34.4 %all-reduce.13.cloned.1.call-done = f32[4,128,64]{1,2,0:T(8,128)} async-done(((f32[4,128,64]{1,2,0:T(8,128)}), f32[4,128,64]{1,2,0:T(8,128)}) %all-reduce.13.cloned.1.call-update) | async-done | bytes 131088 | tf_op jit(solution)/shard_map/psum | solution.py:19
  438.5 8.4 %copy.23 = bf16[256,4,2304]{2,1,0:T(4,128)(2,1)} copy(bf16[256,4,2304]{0,2,1:T(8,128)(2,1)} %get-tuple-element.88) | data formatting | bytes 9437184
  446.9 61.2 %all-reduce.15.cloned.1.call-done = f32[4,128,64]{1,2,0:T(8,128)} async-done(((f32[4,128,64]{1,2,0:T(8,128)}), f32[4,128,64]{1,2,0:T(8,128)}) %all-reduce.15.cloned.1.call-update) | async-done | bytes 131088 | tf_op jit(solution)/shard_map/psum | solution.py:19
  508.6 38.3 %all-reduce.17.cloned.1.call-done = f32[4,128,64]{1,2,0:T(8,128)} async-done(((f32[4,128,64]{1,2,0:T(8,128)}), f32[4,128,64]{1,2,0:T(8,128)}) %all-reduce.17.cloned.1.call-update) | async-done | bytes 131088 | tf_op jit(solution)/shard_map/psum | solution.py:19
  546.9 1.6 copy.55
  (32 shorter events, 4.0 us)
Async XLA Ops:
  7.2 6.0 %copy-start = (s32[4,128,64]{1,2,0:T(8,128)S(1)}, s32[4,128,64]{1,2,0:T(8,128)}, u32[]{:S(2)}) copy-start(s32[4,128,64]{1,2,0:T(8,128)} %param.10) | copy-start | bytes 393220
  7.2 294.7 %all-reduce.7.cloned.1.call-start = ((), (), s32[]{:S(2)}) async-start(), calls=%async_computation | async-start | bytes 9437184 | tf_op jit(solution)/shard_map/psum | solution.py:64
  31.7 270.2 %copy-start.2 = (f32[4,2304]{1,0:T(4,128)S(1)}, f32[4,2304]{1,0:T(4,128)}, u32[]{:S(2)}) copy-start(f32[4,2304]{1,0:T(4,128)} %param.12) | copy-start | bytes 110596
  31.7 325.8 %all-reduce.9.cloned.1.call-start = ((), (), s32[]{:S(2)}) async-start(), calls=%async_computation.1 | async-start | bytes 262144 | tf_op jit(solution)/shard_map/psum | solution.py:19
  324.8 0.7 copy-start.1
  325.5 78.5 %all-reduce.11.cloned.1.call-start = ((), (), s32[]{:S(2)}) async-start(), calls=%async_computation.2 | async-start | bytes 262144 | tf_op jit(solution)/shard_map/psum | solution.py:19
  357.5 80.9 %all-reduce.13.cloned.1.call-start = ((), (), s32[]{:S(2)}) async-start(), calls=%async_computation.3 | async-start | bytes 262144 | tf_op jit(solution)/shard_map/psum | solution.py:19
  404.0 104.0 %all-reduce.15.cloned.1.call-start = ((), (), s32[]{:S(2)}) async-start(), calls=%async_computation.4 | async-start | bytes 262144 | tf_op jit(solution)/shard_map/psum | solution.py:19
  438.4 108.4 %all-reduce.17.cloned.1.call-start = ((), (), s32[]{:S(2)}) async-start(), calls=%async_computation.5 | async-start | bytes 262144 | tf_op jit(solution)/shard_map/psum | solution.py:19
Sparse Core Ops, SparseCore 0:
  31.8 269.9 all-reduce.6
  325.6 31.7 all-reduce.8
  359.9 44.0 all-reduce.10
  406.4 31.9 all-reduce.12
  440.6 67.4 all-reduce.14
  510.6 36.2 all-reduce.16
where the time goes:
time: 556 us; the launch traced here: 555 us
  waiting for transfers between devices  482 us (87%)
  local copies, waits for them, and re-layouts  26.9 us (5%)
  matrix products  20.6 us (4%)
  between operations  14.3 us (3%)
  other arithmetic  10.8 us (2%)
    psum x1, waiting for transfers between devices, on_device(): recon_sum = lax.psum(partials, LAYER_LATENT)  270 us
    psum x5, waiting for transfers between devices, by_axis(): return functools.reduce(lax.psum, axes, x)  212 us
  transfers between devices with their start and end apart: 6, of which 6 were waited for; matrix products, arithmetic and copies ran while one was open for 2% of the time, Pallas kernels for 0%

commit v1 on v0

v1 whole, which is shorter than its diff:
```python
import jax
import jax.numpy as jnp
from jax import lax
from jax.experimental import pallas as pl
from jax.experimental.pallas import tpu as pltpu
from jax.sharding import Mesh
from jax.sharding import PartitionSpec as P

D = 2304
LAYERS = 4
TOPK = 64
TOKENS = 128
SLAB = 256
TILE = 128
PAIRS = D // (2 * TILE)
GROUPS = 3
WIDE = PAIRS // GROUPS
HALF = TOKENS // 2
ROWS = 16
AXES = ("yh", "x", "core", "z", "yl")
MESH = pl.DeviceIdType.MESH
f32 = jnp.float32
bf16 = jnp.bfloat16


def contract(left, right, left_dim, right_dim):
    return lax.dot_general(
        left, right, (((left_dim,), (right_dim,)), ((), ())), preferred_element_type=f32
    )


def here():
    x, core, z = lax.axis_index("x"), lax.axis_index("core"), lax.axis_index("z")
    y = lax.axis_index("yh") * 2 + lax.axis_index("yl")
    return x, y, z, core


def source_layer():
    return lax.axis_index("yh") * 2 + lax.axis_index("x") // 2


def at_x(x):
    return {"x": x}


def at_y(y):
    return {"yh": y // 2, "yl": lax.rem(y, 2)}


def at_z(z):
    return {"z": z}


def slot_of(x, y, core):
    return ((y // 2) * 2 + x // 2) * 8 + lax.rem(y, 2) * 4 + lax.rem(x, 2) * 2 + core


def remote(src, dst, sems, index, device):
    return pltpu.make_async_remote_copy(
        src_ref=src,
        dst_ref=dst,
        send_sem=sems[0].at[index],
        recv_sem=sems[1].at[index],
        device_id=device,
        device_id_type=MESH,
    )


def loop(low, high, body):
    def step(i, carry):
        body(i)
        return carry

    lax.fori_loop(low, high, step, 0)


def exchange_kernel(
    decoder, index_ref, value_ref, bias_ref, target,
    error_out, codes_out, grad_out, square_out,
    weights, spread_codes, forward, own, core_send, core_recv, own_b, target_v,
    recv1, sum1, sum1_b, recv2, sum2, sum2_b, recv3,
    error, squares, square_recv, products, sums, picked, pick_recv, message, plane, gathered,
    weight_sem, target_sem, error_sem,
    core_s, core_r, one_s, one_r, two_s, two_r, three_s, three_r,
    az_s, az_r, sq_s, sq_r, as_s, as_r, af_s, af_r, ac_s, ac_r,
    pz_s, pz_r, pp_s, pp_r, pa_s, pa_r,
):
    x, y, z, core = here()
    source = source_layer()
    offset = ((lax.rem(x, 2) * 2 + core) * 16 + z * 2 + lax.axis_index("yl")) * SLAB
    other = {"core": 1 - core}
    first, second = (x, y), (y, x)
    at_first, at_second = (at_x, at_y), (at_y, at_x)
    tokens_of = [pl.multiple_of(core * HALF + first[p] * ROWS, ROWS) for p in range(2)]

    def weight_copy(tile):
        return pltpu.make_async_copy(
            decoder.at[:, :, pl.ds(tile * TILE, TILE)], weights.at[tile], weight_sem.at[tile]
        )

    def target_copy(p, which):
        tile = (z if which == 0 else PAIRS - 1) * 2 + p
        columns = pl.ds(pl.multiple_of(tile * TILE, TILE), TILE)
        return pltpu.make_async_copy(
            target.at[second[p], pl.ds(tokens_of[p], ROWS), columns],
            target_v.at[p, which],
            target_sem.at[p, which],
        )

    for tile in range(2 * PAIRS):
        weight_copy(tile).start()
    for p in range(2):
        for which in range(2):
            target_copy(p, which).start()

    barrier = pltpu.get_barrier_semaphore()

    def plane_peer(j, sign):
        px = lax.rem(x + 4 + sign * lax.rem(j, 4), 4)
        py = lax.rem(y + 4 + sign * lax.rem(j // 4, 4), 4)
        return px, py, lax.rem(core + j // 16, 2)

    def at_plane(j):
        px, py, pc = plane_peer(j, 1)
        return {"x": px, "core": pc, **at_y(py)}

    def z_peer(i):
        return lax.rem(z + i, 8)

    loop(1, 32, lambda j: pl.semaphore_signal(barrier, inc=1, device_id=at_plane(j), device_id_type=MESH))
    loop(1, 8, lambda i: pl.semaphore_signal(barrier, inc=1, device_id=at_z(z_peer(i)), device_id_type=MESH))

    latents = lax.broadcasted_iota(jnp.int32, (SLAB, TOKENS), 0)

    def place(i, dense):
        part = pl.ds(pl.multiple_of(i * ROWS, ROWS), ROWS)
        columns = index_ref[source, part, :] - offset
        values = value_ref[source, part, :].astype(f32)
        for k in range(ROWS):
            dense = jnp.where(latents == columns[k : k + 1, :], values[k : k + 1, :], dense)
        return dense

    dense = lax.fori_loop(0, TOPK // ROWS, place, jnp.zeros((SLAB, TOKENS), f32)).astype(bf16)
    codes_out[...] = dense
    lane = lax.broadcasted_iota(jnp.int32, (SLAB, LAYERS * SLAB), 1)
    row = lax.broadcasted_iota(jnp.int32, (SLAB, LAYERS * SLAB), 0)
    spread = jnp.where((lane >> 2) == row, 1.0, 0.0).astype(bf16)
    spread_codes[...] = contract(dense, spread, 0, 0)
    lane = lax.broadcasted_iota(jnp.int32, (HALF, LAYERS * SLAB), 1) & 3
    for side in range(2):
        half = spread_codes[pl.ds(pl.multiple_of((core if side == 0 else 1 - core) * HALF, HALF), HALF), :]
        for t in range(LAYERS):
            kept = jnp.where(jnp.logical_and(lane == t, t >= source), half, 0.0)
            forward[(side * LAYERS + t) * HALF : (side * LAYERS + t + 1) * HALF, :] = kept.astype(bf16)

    flat = weights.reshape(2 * PAIRS, LAYERS * SLAB, TILE)

    def core_copy(g):
        part = pl.ds(g * WIDE, WIDE)
        return remote(core_send.at[part], core_recv.at[part], (core_s, core_r), g, other)

    def one_copy(g, p, i):
        part = pl.ds(g * WIDE, WIDE)
        k = lax.rem(first[p] + i, 4)
        rows = pl.ds(pl.multiple_of(k * ROWS, ROWS), ROWS)
        return remote(
            own_b.at[part, p, :, rows, :], recv1.at[p, i - 1, part],
            (one_s, one_r), (p, g, i - 1), at_first[p](k),
        )

    def two_copy(g, p, i):
        part = pl.ds(g * WIDE, WIDE)
        k = lax.rem(second[p] + i, 4)
        return remote(
            sum1_b.at[p, part, k], recv2.at[p, i - 1, part],
            (two_s, two_r), (p, g, i - 1), at_second[p](k),
        )

    def three_copy(p, which, i):
        k = z_peer(i)
        return remote(
            sum2_b.at[p, k if which == 0 else PAIRS - 1], recv3.at[p, i - 1, which],
            (three_s, three_r), (p, which, i - 1), at_z(k),
        )

    def after_core(g):
        core_copy(g).wait_recv()

        def add(i):
            b, p = g * WIDE + i // 2, lax.rem(i, 2)
            total = own[b, p] + core_recv[b, p].astype(f32)
            own[b, p] = total
            own_b[b, p] = total.astype(bf16)

        loop(0, 2 * WIDE, add)
        for i in range(1, 4):
            for p in range(2):
                one_copy(g, p, i).start()

    for g in range(GROUPS):
        for b in range(g * WIDE, (g + 1) * WIDE):
            weight_copy(2 * b).wait()
            weight_copy(2 * b + 1).wait()
            product = contract(forward[...], jnp.concatenate([flat[2 * b], flat[2 * b + 1]], axis=1), 1, 0)
            for p in range(2):
                columns = slice(p * TILE, (p + 1) * TILE)
                own[b, p] = product[: LAYERS * HALF, columns].reshape(LAYERS, HALF, TILE)
                core_send[b, p] = product[LAYERS * HALF :, columns].reshape(LAYERS, HALF, TILE).astype(bf16)
        if g == 0:
            pl.semaphore_wait(barrier, 38)
        core_copy(g).start()
        if g > 0:
            after_core(g - 1)
    after_core(GROUPS - 1)

    for g in range(GROUPS):
        for p in range(2):
            for i in range(1, 4):
                one_copy(g, p, i).wait_recv()

            def add(b):
                total = own[b, p, :, pl.ds(pl.multiple_of(first[p] * ROWS, ROWS), ROWS), :]
                for i in range(3):
                    total = total + recv1[p, i, b].astype(f32)
                sum1[p, b] = total
                sum1_b[p, b] = total.astype(bf16)

            loop(g * WIDE, (g + 1) * WIDE, add)
            for i in range(1, 4):
                two_copy(g, p, i).start()

    for g in range(GROUPS):
        for p in range(2):
            for i in range(1, 4):
                two_copy(g, p, i).wait_recv()

            def add(b):
                total = sum1[p, b, second[p]]
                for i in range(3):
                    total = total + recv2[p, i, b].astype(f32)
                sum2[p, b] = total
                sum2_b[p, b] = total.astype(bf16)

            loop(g * WIDE, (g + 1) * WIDE, add)

    def send_three(i):
        for p in range(2):
            for which in range(2):
                three_copy(p, which, i).start()

    loop(1, 8, send_three)

    tile_row = lax.broadcasted_iota(jnp.int32, (8, TILE), 0)
    layer_row = lax.broadcasted_iota(jnp.int32, (LAYERS, TILE), 0)
    squared = jnp.zeros((8, TILE), f32)

    def z_copy(p, i):
        tile = error.at[z, p, second[p], pl.ds(tokens_of[p], ROWS), :]
        return remote(tile, tile, (az_s, az_r), (p, i - 1), at_z(z_peer(i)))

    def square_copy(i):
        return remote(squares, square_recv.at[z], (sq_s, sq_r), i - 1, at_z(z_peer(i)))

    for p in range(2):
        for which in range(2):
            loop(1, 8, lambda i: three_copy(p, which, i).wait_recv())
            target_copy(p, which).wait()
            tile = z if which == 0 else PAIRS - 1
            total = sum2[p, tile]
            for i in range(7):
                total = total + recv3[p, i, which].astype(f32)
            columns = pl.ds(pl.multiple_of((tile * 2 + p) * TILE, TILE), TILE)
            shift = jnp.sum(jnp.where(layer_row == second[p], bias_ref[:, columns], 0.0), axis=0, keepdims=True)
            residual = total + shift - target_v[p, which].astype(f32)
            error[tile, p, second[p], pl.ds(tokens_of[p], ROWS), :] = residual.astype(bf16)
            square = jnp.sum(residual * residual, axis=0, keepdims=True)
            counted = tile_row == second[p]
            if which == 1:
                counted = jnp.logical_and(counted, z == 0)
            squared = squared + jnp.where(counted, square, 0.0)
            if which == 0:
                loop(1, 8, lambda i: z_copy(p, i).start())
    squares[...] = squared
    square_recv[z] = squared
    loop(1, 8, lambda i: square_copy(i).start())

    def second_copy(p, i):
        tiles = error.at[:, p, second[p], pl.ds(tokens_of[p], ROWS), :]
        return remote(tiles, tiles, (as_s, as_r), (p, i - 1), at_second[p](lax.rem(second[p] + i, 4)))

    def first_copy(g, p, i):
        tiles = error.at[pl.ds(g * WIDE, WIDE), p, :, pl.ds(tokens_of[p], ROWS), :]
        return remote(tiles, tiles, (af_s, af_r), (p, g, i - 1), at_first[p](lax.rem(first[p] + i, 4)))

    def half_copy(g):
        tiles = error.at[pl.ds(g * WIDE, WIDE), :, :, pl.ds(pl.multiple_of(core * HALF, HALF), HALF), :]
        return remote(tiles, tiles, (ac_s, ac_r), g, other)

    def error_copy(g):
        part = pl.ds(g * WIDE, WIDE)
        return pltpu.make_async_copy(error.at[part], error_out.at[part], error_sem.at[g])

    for p in range(2):
        loop(1, 8, lambda i: z_copy(p, i).wait_recv())
        for i in range(1, 4):
            second_copy(p, i).start()
    for p in range(2):
        for i in range(1, 4):
            second_copy(p, i).wait_recv()
    for g in range(GROUPS):
        for i in range(1, 4):
            for p in range(2):
                first_copy(g, p, i).start()
    for g in range(GROUPS):
        for p in range(2):
            for i in range(1, 4):
                first_copy(g, p, i).wait_recv()
        half_copy(g).start()
        if g > 0:
            backward(g - 1, half_copy, error_copy, flat, error, products)
    backward(GROUPS - 1, half_copy, error_copy, flat, error, products)

    total = jnp.zeros((SLAB, TOKENS), f32)
    for t in range(LAYERS):
        total = total + jnp.where(t >= source, products[t, pl.ds(t, SLAB, stride=LAYERS), :], 0.0)
    sums[...] = total
    columns = index_ref[source] - offset

    def pick(i, out):
        rows = sums[pl.ds(pl.multiple_of(i * 8, 8), 8), :]
        for r in range(8):
            out = jnp.where(columns == i * 8 + r, rows[r : r + 1, :], out)
        return out

    picked[...] = lax.fori_loop(0, SLAB // 8, pick, jnp.zeros((TOPK, TOKENS), f32))

    def pick_copy(i):
        k = z_peer(i)
        rows = picked.at[pl.ds(pl.multiple_of(k * 8, 8), 8), :]
        return remote(rows, pick_recv.at[i - 1], (pz_s, pz_r), i - 1, at_z(k))

    my_slot = slot_of(x, y, core)
    z_rows = pl.ds(pl.multiple_of(z * 8, 8), 8)

    def plane_copy(j):
        return remote(message, plane.at[my_slot], (pp_s, pp_r), j - 1, at_plane(j))

    def plane_arrival(j):
        return remote(message, plane.at[slot_of(*plane_peer(j, -1))], (pp_s, pp_r), j - 1, at_plane(j))

    def gather_copy(i):
        rows = gathered.at[:, z_rows, :]
        return remote(rows, rows, (pa_s, pa_r), i - 1, at_z(z_peer(i)))

    loop(1, 8, lambda i: pick_copy(i).start())
    loop(1, 8, lambda i: square_copy(i).wait_recv())
    total = square_recv[0]
    for i in range(1, 8):
        total = total + square_recv[i]
    message[1] = total
    loop(1, 8, lambda i: pick_copy(i).wait_recv())
    total = picked[z_rows, :]
    for i in range(7):
        total = total + pick_recv[i]
    message[0] = total
    plane[my_slot] = message[...]
    loop(1, 32, lambda j: plane_copy(j).start())
    loop(1, 32, lambda j: plane_arrival(j).wait_recv())
    squared = jnp.zeros((8, TILE), f32)
    for s in range(LAYERS):
        total = plane[s * 8, 0]
        squared = squared + plane[s * 8, 1]
        for i in range(1, 8):
            total = total + plane[s * 8 + i, 0]
            squared = squared + plane[s * 8 + i, 1]
        gathered[s, z_rows, :] = total
    loop(1, 8, lambda i: gather_copy(i).start())
    square_out[...] = squared

    for g in range(GROUPS):
        core_copy(g).wait_send()
        half_copy(g).wait_send()
        error_copy(g).wait()
        for p in range(2):
            for i in range(1, 4):
                one_copy(g, p, i).wait_send()
                two_copy(g, p, i).wait_send()
                first_copy(g, p, i).wait_send()
    for p in range(2):
        for i in range(1, 4):
            second_copy(p, i).wait_send()

    def z_sent(i):
        for p in range(2):
            z_copy(p, i).wait_send()
            for which in range(2):
                three_copy(p, which, i).wait_send()
        square_copy(i).wait_send()
        pick_copy(i).wait_send()

    loop(1, 8, z_sent)
    loop(1, 32, lambda j: plane_copy(j).wait_send())
    loop(1, 8, lambda i: gather_copy(i).wait())
    grad_out[...] = gathered[...]


def backward(g, half_copy, error_copy, flat, error, products):
    half_copy(g).wait_recv()
    error_copy(g).start()
    left, right = [], []
    for b in range(g * WIDE, (g + 1) * WIDE):
        for p in range(2):
            left.append(flat[2 * b + p])
            right.append(error[b, p].reshape(LAYERS * TOKENS, TILE))
    product = contract(jnp.concatenate(left, axis=1), jnp.concatenate(right, axis=1), 1, 1)
    for t in range(LAYERS):
        block = product[:, t * TILE : (t + 1) * TILE]
        products[t] = block if g == 0 else products[t] + block


def grads_kernel(codes_ref, error_ref, grads, spread, staged, sems):
    source = source_layer()
    row = lax.broadcasted_iota(jnp.int32, (LAYERS * SLAB, SLAB), 0)
    lane = lax.broadcasted_iota(jnp.int32, (LAYERS * SLAB, SLAB), 1)
    pattern = jnp.where((row >> 2) == lane, 1.0, 0.0).astype(bf16)
    wide = contract(pattern, codes_ref[...], 1, 0)
    row = lax.broadcasted_iota(jnp.int32, (LAYERS * SLAB, TOKENS), 0) & 3
    for t in range(LAYERS):
        kept = jnp.where(jnp.logical_and(row == t, t >= source), wide, 0.0)
        spread[:, t * TOKENS : (t + 1) * TOKENS] = kept.astype(bf16)
    flat = staged.reshape(2 * PAIRS, LAYERS * SLAB, TILE)

    def out_copy(tile):
        return pltpu.make_async_copy(
            staged.at[tile], grads.at[:, :, pl.ds(tile * TILE, TILE)], sems.at[tile]
        )

    for b in range(PAIRS):
        both = [error_ref[b, p].reshape(LAYERS * TOKENS, TILE) for p in range(2)]
        product = contract(spread[...], jnp.concatenate(both, axis=1), 1, 0).astype(bf16)
        for p in range(2):
            flat[2 * b + p] = product[:, p * TILE : (p + 1) * TILE]
            out_copy(2 * b + p).start()
    for tile in range(2 * PAIRS):
        out_copy(tile).wait()


def on_device(decoder, code_index, code_value, bias, target):
    in_vmem = pl.BlockSpec(memory_space=pltpu.VMEM)
    anywhere = pl.BlockSpec(memory_space=pl.ANY)

    def shape(*dims):
        return lambda dtype: pltpu.VMEM(dims, dtype)

    def sems(*dims):
        return pltpu.SemaphoreType.DMA(dims)

    errors = (PAIRS, 2, LAYERS, TOKENS, TILE)
    error_b, codes, grad, squares = pl.pallas_call(
        exchange_kernel,
        name="exchange",
        out_shape=(
            jax.ShapeDtypeStruct(errors, bf16),
            jax.ShapeDtypeStruct((SLAB, TOKENS), bf16),
            jax.ShapeDtypeStruct((LAYERS, TOPK, TOKENS), f32),
            jax.ShapeDtypeStruct((8, TILE), f32),
        ),
        in_specs=[anywhere, in_vmem, in_vmem, in_vmem, anywhere],
        out_specs=(anywhere, in_vmem, in_vmem, in_vmem),
        scratch_shapes=[
            pltpu.VMEM((2 * PAIRS, SLAB, LAYERS, TILE), bf16),
            pltpu.VMEM((TOKENS, LAYERS * SLAB), f32),
            pltpu.VMEM((LAYERS * TOKENS, LAYERS * SLAB), bf16),
            pltpu.VMEM((PAIRS, 2, LAYERS, HALF, TILE), f32),
            pltpu.VMEM((PAIRS, 2, LAYERS, HALF, TILE), bf16),
            pltpu.VMEM((PAIRS, 2, LAYERS, HALF, TILE), bf16),
            pltpu.VMEM((PAIRS, 2, LAYERS, HALF, TILE), bf16),
            pltpu.VMEM((2, 2, ROWS, TILE), bf16),
            pltpu.VMEM((2, 3, PAIRS, LAYERS, ROWS, TILE), bf16),
            pltpu.VMEM((2, PAIRS, LAYERS, ROWS, TILE), f32),
            pltpu.VMEM((2, PAIRS, LAYERS, ROWS, TILE), bf16),
            pltpu.VMEM((2, 3, PAIRS, ROWS, TILE), bf16),
            pltpu.VMEM((2, PAIRS, ROWS, TILE), f32),
            pltpu.VMEM((2, PAIRS, ROWS, TILE), bf16),
            pltpu.VMEM((2, 7, 2, ROWS, TILE), bf16),
            pltpu.VMEM(errors, bf16),
            pltpu.VMEM((8, TILE), f32),
            pltpu.VMEM((8, 8, TILE), f32),
            pltpu.VMEM((LAYERS, LAYERS * SLAB, TOKENS), f32),
            pltpu.VMEM((SLAB, TOKENS), f32),
            pltpu.VMEM((TOPK, TOKENS), f32),
            pltpu.VMEM((7, 8, TILE), f32),
            pltpu.VMEM((2, 8, TILE), f32),
            pltpu.VMEM((32, 2, 8, TILE), f32),
            pltpu.VMEM((LAYERS, TOPK, TOKENS), f32),
            sems(2 * PAIRS), sems(2, 2), sems(GROUPS),
            sems(GROUPS), sems(GROUPS), sems(2, GROUPS, 3), sems(2, GROUPS, 3),
            sems(2, GROUPS, 3), sems(2, GROUPS, 3), sems(2, 2, 7), sems(2, 2, 7),
            sems(2, 7), sems(2, 7), sems(7), sems(7), sems(2, 3), sems(2, 3),
            sems(2, GROUPS, 3), sems(2, GROUPS, 3), sems(GROUPS), sems(GROUPS),
            sems(7), sems(7), sems(31), sems(31), sems(7), sems(7),
        ],
        compiler_params=pltpu.CompilerParams(
            collective_id=0, has_side_effects=True, vmem_limit_bytes=44 << 20
        ),
    )(
        decoder,
        jnp.transpose(code_index, (0, 2, 1)),
        jnp.transpose(code_value, (0, 2, 1)),
        bias,
        target,
    )
    grads = pl.pallas_call(
        grads_kernel,
        name="decoder_gradient",
        out_shape=jax.ShapeDtypeStruct(decoder.shape, bf16),
        in_specs=[in_vmem, in_vmem],
        out_specs=anywhere,
        scratch_shapes=[
            pltpu.VMEM((LAYERS * SLAB, LAYERS * TOKENS), bf16),
            pltpu.VMEM((2 * PAIRS, SLAB, LAYERS, TILE), bf16),
            sems(2 * PAIRS),
        ],
        compiler_params=pltpu.CompilerParams(vmem_limit_bytes=32 << 20),
    )(codes, error_b)
    layer_error = jnp.sum(squares[:LAYERS], axis=1) / (TOKENS * D)
    return layer_error, grads, jnp.transpose(grad, (0, 2, 1))


def solution(mesh):
    torus = Mesh(mesh.devices.reshape(2, 4, 2, 8, 2), AXES)
    rows = P(AXES, None, None)
    return jax.shard_map(
        on_device,
        mesh=torus,
        in_specs=(rows, P(), P(), P(), P()),
        out_specs=(P(), rows, P()),
        check_vma=False,
    )
```

time: 556 us -> 88.1 us (0.16)
  waiting for transfers between devices: 482 us -> 0 us
  Pallas kernels: 0 us -> 79.3 us
  matrix products: 20.6 us -> 0 us
  local copies, waits for them, and re-layouts: 26.9 us -> 7.16 us
  between operations: 14.3 us -> 0.66 us
  other arithmetic: 10.8 us -> 0.63 us
    psum x6 -> x0, waiting for transfers between devices: 482 us -> none  [the longest x1 270 us: on_device(): recon_sum = lax.psum(partials, LAYER_LATENT)]
    pallas_call x0 -> x2, Pallas kernels: none -> 79.3 us  [the longest x1 74.3 us: on_device(): pl.pallas_call(exchange_kernel, name='exchange', out_shape=(jax.ShapeDtyp...]
    dot_general x12 -> x0, matrix products: 20.6 us -> none  [the longest x4 7.25 us: contract_cols(): lax.dot_general(left, right, (((1,), (1,)), ((), ())), preferred_element_...]
    dynamic_update_slice x9 -> x0, local copies, waits for them, and re-layouts: 5.85 us -> none  [the longest x8 5.84 us: forward_step(): return lax.dynamic_update_index_in_dim(totals, product, target_layer, 0)]
  transfers between devices with their start and end apart: 6 -> 0, of which waited for: 6 -> 0; matrix products, arithmetic and copies ran while one was open for 2% -> 0% of each run, Pallas kernels for 0% -> 0%
where the time goes in v1:
time: 88.1 us; the launch traced here: 87.8 us
  Pallas kernels  79.3 us (90%)
  local copies, waits for them, and re-layouts  7.16 us (8%)
    pallas_call x1, Pallas kernels, on_device(): pl.pallas_call(exchange_kernel, name='exchange', out_shape=(jax.ShapeDtyp...  74.3 us
    unnamed x11, local copies, waits for them, and re-layouts  7.16 us
    pallas_call x1, Pallas kernels, on_device(): pl.pallas_call(grads_kernel, name='decoder_gradient', out_shape=jax.Shape...  5.03 us

profile of v1, /device:TPU:1, one launch (start us, length us, event | category | flops | bytes accessed | tf_op | source)
XLA Modules:
  0.0 87.8 jit_solution(12541706347920402581)
XLA Ops:
  0.6 0.0 copy-start
  0.6 2.3 %copy-done = bf16[256,4,2304]{2,1,0:T(4,128)(2,1)S(1)} copy-done((bf16[256,4,2304]{2,1,0:T(4,128)(2,1)S(1)}, bf16[256,4,2304]{2,1,0:T(4,128)(2,1)}, u32[]{:S(2)}) %copy-start) | copy-done | bytes 4718616
  3.0 0.0 copy-start.1
  3.0 1.7 %copy-done.1 = bf16[4,128,2304]{2,1,0:T(8,128)(2,1)S(1)} copy-done((bf16[4,128,2304]{2,1,0:T(8,128)(2,1)S(1)}, bf16[4,128,2304]{2,1,0:T(8,128)(2,1)}, u32[]{:S(2)}) %copy-start.1) | copy-done | bytes 2359320
  4.6 0.0 copy-start.2
  4.6 0.9 %copy-done.2 = s32[4,128,64]{1,2,0:T(8,128)S(1)} copy-done((s32[4,128,64]{1,2,0:T(8,128)S(1)}, s32[4,128,64]{1,2,0:T(8,128)}, u32[]{:S(2)}) %copy-start.2) | copy-done | bytes 131096
  5.5 0.0 copy-start.3
  5.5 0.8 copy-done.3
  6.4 0.0 copy-start.4
  6.4 0.8 copy-done.4
  7.1 74.3 %exchange.1 = (bf16[9,2,4,128,128]{4,3,2,1,0:T(8,128)(2,1)S(1)}, bf16[256,128]{1,0:T(8,128)(2,1)S(1)}, f32[4,64,128]{2,1,0:T(8,128)S(1)}, f32[8,128]{1,0:T(8,128)S(1)}) custom-call(bf16[256,4,2304]{2,1,0:T(4,128)(2,1)S(1)} %copy-done, s32[4,64,128]{2,1,0:T(8,128)S(1)} %bitcast.3, bf16[4,64,128]{2,1,0:T(8,128)(2,1)S(1)} %bitcast.5, f32[4,2304]{1,0:T(4,128)S(1)} %copy-done.4, ...), custom_call_target="tpu_custom_call" | custom-call | tf_op jit(solution)/shard_map/exchange/pallas_call | solution.py:459
  81.4 0.1 slice_reduce_fusion
  81.6 0.5 broadcast_multiply_fusion
  82.1 5.0 %decoder_gradient.1 = bf16[256,4,2304]{2,1,0:T(4,128)(2,1)} custom-call(bf16[256,128]{1,0:T(8,128)(2,1)S(1)} %get-tuple-element.8.codes_ref, bf16[9,2,4,128,128]{4,3,2,1,0:T(8,128)(2,1)S(1)} %get-tuple-element.9.error_ref), custom_call_target="tpu_custom_call" | custom-call | tf_op jit(solution)/shard_map/decoder_gradient/pallas_call | solution.py:513
  87.1 0.7 copy.9
Async XLA Ops:
  0.6 2.3 %copy-start = (bf16[256,4,2304]{2,1,0:T(4,128)(2,1)S(1)}, bf16[256,4,2304]{2,1,0:T(4,128)(2,1)}, u32[]{:S(2)}) copy-start(bf16[256,4,2304]{2,1,0:T(4,128)(2,1)} %decoder.1) | copy-start | bytes 14155780
  3.0 1.7 %copy-start.1 = (bf16[4,128,2304]{2,1,0:T(8,128)(2,1)S(1)}, bf16[4,128,2304]{2,1,0:T(8,128)(2,1)}, u32[]{:S(2)}) copy-start(bf16[4,128,2304]{2,1,0:T(8,128)(2,1)} %target.1) | copy-start | bytes 7077892
  4.6 0.9 %copy-start.2 = (s32[4,128,64]{1,2,0:T(8,128)S(1)}, s32[4,128,64]{1,2,0:T(8,128)}, u32[]{:S(2)}) copy-start(s32[4,128,64]{1,2,0:T(8,128)} %param.6) | copy-start | bytes 393220
  5.5 0.8 copy-start.3
  6.4 0.8 copy-start.4

commit v2 on v1

v2 whole, which is shorter than its diff:
```python
import functools

import jax
import jax.numpy as jnp
from jax import lax
from jax.experimental import pallas as pl
from jax.experimental.pallas import tpu as pltpu
from jax.sharding import Mesh
from jax.sharding import PartitionSpec as P

D = 2304
LAYERS = 4
TOPK = 64
TOKENS = 128
SLAB = 256
TILE = 128
PAIRS = D // (2 * TILE)
GROUPS = 3
WIDE = PAIRS // GROUPS
HALF = TOKENS // 2
ROWS = 16
AXES = ("yh", "x", "core", "z", "yl")
MESH = pl.DeviceIdType.MESH
f32 = jnp.float32
bf16 = jnp.bfloat16


def contract(left, right, left_dim, right_dim):
    return lax.dot_general(
        left, right, (((left_dim,), (right_dim,)), ((), ())), preferred_element_type=f32
    )


def here():
    x, core, z = lax.axis_index("x"), lax.axis_index("core"), lax.axis_index("z")
    y = lax.axis_index("yh") * 2 + lax.axis_index("yl")
    return x, y, z, core


def source_layer():
    return lax.axis_index("yh") * 2 + lax.axis_index("x") // 2


def at_x(x):
    return {"x": x}


def at_y(y):
    return {"yh": y // 2, "yl": lax.rem(y, 2)}


def at_z(z):
    return {"z": z}


def remote(src, dst, sems, index, device):
    return pltpu.make_async_remote_copy(
        src_ref=src,
        dst_ref=dst,
        send_sem=sems[0].at[index],
        recv_sem=sems[1].at[index],
        device_id=device,
        device_id_type=MESH,
    )


def waits(low, high, copy):
    return lambda: loop(low, high, lambda i: copy(i).wait_send())


def loop(low, high, body):
    def step(i, carry):
        body(i)
        return carry

    lax.fori_loop(low, high, step, 0)


def exchange_kernel(
    decoder, index_hbm, value_hbm, bias_hbm, target,
    grads_out, grad_out, square_out,
    weights, index_ref, value_ref, bias_ref, spread_codes, forward, own, core_send, core_recv, own_b, target_v,
    recv1, sum1, sum1_b, recv2, sum2, sum2_b, recv3,
    error, codes, wide_codes, squares, products, sums, picked, pick_recv, by_z, by_plane,
    small_sem, weight_sem, target_sem,
    core_s, core_r, one_s, one_r, two_s, two_r, three_s, three_r,
    as_s, as_r, af_s, af_r, ac_s, ac_r,
    az_s, az_r, pn_s, pn_r, pz_s, pz_r, pp_s, pp_r, pc_s, pc_r,
):
    x, y, z, core = here()
    source = source_layer()
    offset = ((lax.rem(x, 2) * 2 + core) * 16 + z * 2 + lax.axis_index("yl")) * SLAB
    other = {"core": 1 - core}
    pending = []
    first, second = (x, y), (y, x)
    at_first, at_second = (at_x, at_y), (at_y, at_x)
    tokens_of = [pl.multiple_of(core * HALF + first[p] * ROWS, ROWS) for p in range(2)]

    def group(g):
        return pl.ds(g * WIDE, WIDE)

    def weight_copy(tile):
        return pltpu.make_async_copy(
            decoder.at[:, :, pl.ds(tile * TILE, TILE)], weights.at[tile], weight_sem.at[tile]
        )

    def target_copy(p, which):
        tile = (z if which == 0 else PAIRS - 1) * 2 + p
        columns = pl.ds(pl.multiple_of(tile * TILE, TILE), TILE)
        return pltpu.make_async_copy(
            target.at[second[p], pl.ds(tokens_of[p], ROWS), columns],
            target_v.at[p, which],
            target_sem.at[p, which],
        )

    barrier = pltpu.get_barrier_semaphore()

    def z_peer(i):
        return lax.rem(z + i, 8)

    def at_plane(i):
        return {"x": lax.rem(x + lax.rem(i, 4), 4), **at_y(lax.rem(y + i // 4, 4))}

    def flip(position, by):
        return position + by * (1 - 2 * lax.rem(position, 2))

    def near(i):
        return flip(x, lax.rem(i, 2)), flip(y, lax.rem(i // 2, 2)), flip(core, i // 4)

    def at_near(i):
        px, py, pc = near(i)
        return {"x": px, "core": pc, **at_y(py)}

    def greet(device):
        pl.semaphore_signal(barrier, inc=1, device_id=device, device_id_type=MESH)

    loop(1, 8, lambda i: greet(at_z(z_peer(i))))
    loop(1, 16, lambda i: greet(at_plane(i)))
    loop(4, 8, lambda i: greet(at_near(i)))

    small = [
        pltpu.make_async_copy(index_hbm.at[source], index_ref, small_sem.at[0]),
        pltpu.make_async_copy(value_hbm.at[source], value_ref, small_sem.at[1]),
        pltpu.make_async_copy(bias_hbm, bias_ref, small_sem.at[2]),
    ]
    for copy in small:
        copy.start()
    for tile in range(2 * PAIRS):
        weight_copy(tile).start()
    for p in range(2):
        for which in range(2):
            target_copy(p, which).start()

    for copy in small:
        copy.wait()
    latents = lax.broadcasted_iota(jnp.int32, (SLAB, TOKENS), 0)

    def place(i, dense):
        part = pl.ds(pl.multiple_of(i * ROWS, ROWS), ROWS)
        columns = index_ref[part, :] - offset
        values = value_ref[part, :].astype(f32)
        for k in range(ROWS):
            dense = jnp.where(latents == columns[k : k + 1, :], values[k : k + 1, :], dense)
        return dense

    dense = lax.fori_loop(0, TOPK // ROWS, place, jnp.zeros((SLAB, TOKENS), f32)).astype(bf16)
    codes[...] = dense
    lane = lax.broadcasted_iota(jnp.int32, (SLAB, LAYERS * SLAB), 1)
    row = lax.broadcasted_iota(jnp.int32, (SLAB, LAYERS * SLAB), 0)
    spread = jnp.where((lane >> 2) == row, 1.0, 0.0).astype(bf16)
    spread_codes[...] = contract(dense, spread, 0, 0)
    lane = lax.broadcasted_iota(jnp.int32, (HALF, LAYERS * SLAB), 1) & 3
    for side in range(2):
        half = spread_codes[pl.ds(pl.multiple_of((core if side == 0 else 1 - core) * HALF, HALF), HALF), :]
        for t in range(LAYERS):
            kept = jnp.where(jnp.logical_and(lane == t, t >= source), half, 0.0)
            forward[(side * LAYERS + t) * HALF : (side * LAYERS + t + 1) * HALF, :] = kept.astype(bf16)

    flat = weights.reshape(2 * PAIRS, LAYERS * SLAB, TILE)

    def core_copy(g):
        return remote(core_send.at[group(g)], core_recv.at[group(g)], (core_s, core_r), g, other)

    def one_copy(g, p, i):
        k = lax.rem(first[p] + i, 4)
        rows = pl.ds(pl.multiple_of(k * ROWS, ROWS), ROWS)
        return remote(
            own_b.at[group(g), p, :, rows, :], recv1.at[p, i - 1, group(g)],
            (one_s, one_r), (p, g, i - 1), at_first[p](k),
        )

    def two_copy(g, p, i):
        k = lax.rem(second[p] + i, 4)
        return remote(
            sum1_b.at[p, group(g), k], recv2.at[p, i - 1, group(g)],
            (two_s, two_r), (p, g, i - 1), at_second[p](k),
        )

    def three_copy(p, which, i):
        k = z_peer(i)
        return remote(
            sum2_b.at[p, k if which == 0 else PAIRS - 1], recv3.at[p, i - 1, which],
            (three_s, three_r), (p, which, i - 1), at_z(k),
        )

    def z_copy(p, i):
        tile = error.at[z, p, second[p], pl.ds(tokens_of[p], ROWS), :]
        return remote(tile, tile, (az_s, az_r), (p, i - 1), at_z(z_peer(i)))

    def second_copy(p, i):
        tiles = error.at[:, p, second[p], pl.ds(tokens_of[p], ROWS), :]
        return remote(tiles, tiles, (as_s, as_r), (p, i - 1), at_second[p](lax.rem(second[p] + i, 4)))

    def first_copy(g, p, i):
        tiles = error.at[group(g), p, :, pl.ds(tokens_of[p], ROWS), :]
        return remote(tiles, tiles, (af_s, af_r), (p, g, i - 1), at_first[p](lax.rem(first[p] + i, 4)))

    def half_copy(g):
        tiles = error.at[group(g), :, :, pl.ds(pl.multiple_of(core * HALF, HALF), HALF), :]
        return remote(tiles, tiles, (ac_s, ac_r), g, other)

    def exchange(copy, g):
        for i in range(1, 4):
            for p in range(2):
                copy(g, p, i).start()
                pending.append(copy(g, p, i).wait_send)

    def arrive(copy, g):
        for p in range(2):
            for i in range(1, 4):
                copy(g, p, i).wait_recv()

    def add_core(g):
        core_copy(g).wait_recv()

        def add(i):
            b, p = g * WIDE + i // 2, lax.rem(i, 2)
            total = own[b, p] + core_recv[b, p].astype(f32)
            own[b, p] = total
            own_b[b, p] = total.astype(bf16)

        loop(0, 2 * WIDE, add)
        exchange(one_copy, g)

    def add_first(g):
        arrive(one_copy, g)
        for p in range(2):

            def add(b):
                total = own[b, p, :, pl.ds(pl.multiple_of(first[p] * ROWS, ROWS), ROWS), :]
                for i in range(3):
                    total = total + recv1[p, i, b].astype(f32)
                sum1[p, b] = total
                sum1_b[p, b] = total.astype(bf16)

            loop(g * WIDE, (g + 1) * WIDE, add)
        exchange(two_copy, g)

    def add_second(g):
        arrive(two_copy, g)
        for p in range(2):

            def add(b):
                total = sum1[p, b, second[p]]
                for k in range(3):
                    total = total + recv2[p, k, b].astype(f32)
                sum2[p, b] = total
                sum2_b[p, b] = total.astype(bf16)

            loop(g * WIDE, (g + 1) * WIDE, add)

    def add_z():
        def send(i):
            for p in range(2):
                for which in range(2):
                    three_copy(p, which, i).start()

        loop(1, 8, send)
        pending.extend(waits(1, 8, functools.partial(three_copy, p, which)) for p in range(2) for which in range(2))

    layer_row = lax.broadcasted_iota(jnp.int32, (LAYERS, TILE), 0)
    tile_row = lax.broadcasted_iota(jnp.int32, (8, TILE), 0)

    def take_errors():
        squared = jnp.zeros((8, TILE), f32)
        for which in range(2):
            for p in range(2):
                loop(1, 8, lambda i: three_copy(p, which, i).wait_recv())
                target_copy(p, which).wait()
                tile = z if which == 0 else PAIRS - 1
                total = sum2[p, tile]
                for i in range(7):
                    total = total + recv3[p, i, which].astype(f32)
                columns = pl.ds(pl.multiple_of((tile * 2 + p) * TILE, TILE), TILE)
                shift = jnp.sum(jnp.where(layer_row == second[p], bias_ref[:, columns], 0.0), axis=0, keepdims=True)
                residual = total + shift - target_v[p, which].astype(f32)
                error[tile, p, second[p], pl.ds(tokens_of[p], ROWS), :] = residual.astype(bf16)
                if which == 0:
                    loop(1, 8, lambda i: z_copy(p, i).start())
                    pending.append(waits(1, 8, functools.partial(z_copy, p)))
                square = jnp.sum(residual * residual, axis=0, keepdims=True)
                counted = tile_row == second[p]
                if which == 1:
                    counted = jnp.logical_and(counted, z == 0)
                squared = squared + jnp.where(counted, square, 0.0)
        squares[...] = squared

    def pass_layers():
        for p in range(2):
            loop(1, 8, lambda i: z_copy(p, i).wait_recv())
            for i in range(1, 4):
                second_copy(p, i).start()
                pending.append(second_copy(p, i).wait_send)
        for p in range(2):
            for i in range(1, 4):
                second_copy(p, i).wait_recv()

    def pass_rows(g):
        arrive(first_copy, g)
        half_copy(g).start()
        pending.append(half_copy(g).wait_send)

    def backward(g):
        half_copy(g).wait_recv()
        left, right = [], []
        for b in range(g * WIDE, (g + 1) * WIDE):
            for p in range(2):
                left.append(flat[2 * b + p])
                right.append(error[b, p].reshape(LAYERS * TOKENS, TILE))
        product = contract(jnp.concatenate(left, axis=1), jnp.concatenate(right, axis=1), 1, 1)
        for t in range(LAYERS):
            block = product[:, t * TILE : (t + 1) * TILE]
            products[t] = block if g == 0 else products[t] + block

    def project(g):
        for tile in range(2 * g * WIDE, 2 * (g + 1) * WIDE):
            weight_copy(tile).wait()
        for b in range(g * WIDE, (g + 1) * WIDE):
            product = contract(forward[...], jnp.concatenate([flat[2 * b], flat[2 * b + 1]], axis=1), 1, 0)
            for p in range(2):
                columns = slice(p * TILE, (p + 1) * TILE)
                own[b, p] = product[: LAYERS * HALF, columns].reshape(LAYERS, HALF, TILE)
                core_send[b, p] = product[LAYERS * HALF :, columns].reshape(LAYERS, HALF, TILE).astype(bf16)

    def send_core(g):
        core_copy(g).start()
        pending.append(core_copy(g).wait_send)

    project(0)
    project(1)
    pl.semaphore_wait(barrier, 26)
    send_core(0)
    send_core(1)
    project(2)
    send_core(2)
    for stage in (add_core, add_first, add_second):
        for g in range(GROUPS):
            stage(g)
    add_z()
    pattern_row = lax.broadcasted_iota(jnp.int32, (LAYERS * SLAB, SLAB), 0)
    pattern_lane = lax.broadcasted_iota(jnp.int32, (LAYERS * SLAB, SLAB), 1)
    pattern = jnp.where((pattern_row >> 2) == pattern_lane, 1.0, 0.0).astype(bf16)
    tall = contract(pattern, codes[...], 1, 0)
    pattern_row = lax.broadcasted_iota(jnp.int32, (LAYERS * SLAB, TOKENS), 0) & 3
    for t in range(LAYERS):
        kept = jnp.where(jnp.logical_and(pattern_row == t, t >= source), tall, 0.0)
        wide_codes[:, t * TOKENS : (t + 1) * TOKENS] = kept.astype(bf16)
    take_errors()
    pass_layers()
    for g in range(GROUPS):
        exchange(first_copy, g)
    for g in range(GROUPS):
        pass_rows(g)
        if g > 0:
            backward(g - 1)
    backward(GROUPS - 1)

    total = jnp.zeros((SLAB, TOKENS), f32)
    for t in range(LAYERS):
        total = total + jnp.where(t >= source, products[t, pl.ds(t, SLAB, stride=LAYERS), :], 0.0)
    sums[...] = total
    columns = index_ref[...] - offset

    def pick(i, out):
        rows = sums[pl.ds(pl.multiple_of(i * 8, 8), 8), :]
        for r in range(8):
            out = jnp.where(columns == i * 8 + r, rows[r : r + 1, :], out)
        return out

    picked[...] = lax.fori_loop(0, SLAB // 8, pick, jnp.zeros((TOPK, TOKENS), f32))

    flat_out = grads_out.reshape(2 * PAIRS, LAYERS * SLAB, TILE)

    def decoder_gradients(g):
        for b in range(g * WIDE, (g + 1) * WIDE):
            both = [error[b, p].reshape(LAYERS * TOKENS, TILE) for p in range(2)]
            product = contract(wide_codes[...], jnp.concatenate(both, axis=1), 1, 0).astype(bf16)
            for p in range(2):
                flat_out[2 * b + p] = product[:, p * TILE : (p + 1) * TILE]

    def rank(px, py, pc):
        return lax.rem(px, 2) + 2 * lax.rem(py, 2) + 4 * pc

    def near_copy(i):
        rows = picked.at[pl.ds(pl.multiple_of(rank(*near(i)) * 8, 8), 8), :]
        return remote(rows, pick_recv.at[i - 1], (pn_s, pn_r), i - 1, at_near(i))

    def sum_copy(i):
        return remote(by_z.at[z], by_z.at[z], (pz_s, pz_r), i - 1, at_z(z_peer(i)))

    def plane_copy(i):
        mine = by_plane.at[core, y * 4 + x]
        return remote(mine, mine, (pp_s, pp_r), i - 1, at_plane(i))

    def pair_copy():
        return remote(by_plane.at[core], by_plane.at[core], (pc_s, pc_r), 0, other)

    loop(1, 8, lambda i: near_copy(i).start())
    pending.append(waits(1, 8, near_copy))
    decoder_gradients(0)
    loop(1, 8, lambda i: near_copy(i).wait_recv())
    total = picked[pl.ds(pl.multiple_of(rank(x, y, core) * 8, 8), 8), :]
    for i in range(7):
        total = total + pick_recv[i]
    by_z[z, 0] = total
    by_z[z, 1] = squares[...]
    loop(1, 8, lambda i: sum_copy(i).start())
    pending.append(waits(1, 8, sum_copy))
    decoder_gradients(1)
    loop(1, 8, lambda i: sum_copy(i).wait_recv())
    total = by_z[0]
    for i in range(1, 8):
        total = total + by_z[i]
    by_plane[core, y * 4 + x] = total
    loop(1, 16, lambda i: plane_copy(i).start())
    pending.append(waits(1, 16, plane_copy))
    decoder_gradients(2)
    loop(1, 16, lambda i: plane_copy(i).wait_recv())
    pair_copy().start()
    pending.append(pair_copy().wait_send)
    for wait in pending[:-1]:
        wait()
    pair_copy().wait_recv()
    squared = jnp.zeros((8, TILE), f32)
    for pc in range(2):
        for py in range(4):
            for px in range(4):
                at = (px % 2 + 2 * (py % 2) + 4 * pc) * 8
                grad_out[py // 2 * 2 + px // 2, at : at + 8, :] = by_plane[pc, py * 4 + px, 0]
                squared = squared + by_plane[pc, py * 4 + px, 1]
    square_out[...] = squared
    pending[-1]()


def layout_kernel(grads, out, sems):
    copies = [
        pltpu.make_async_copy(grads.at[tile], out.at[:, :, pl.ds(tile * TILE, TILE)], sems.at[tile])
        for tile in range(2 * PAIRS)
    ]
    for copy in copies:
        copy.start()
    for copy in copies:
        copy.wait()


def on_device(decoder, code_index, code_value, bias, target):
    in_vmem = pl.BlockSpec(memory_space=pltpu.VMEM)
    in_hbm = pl.BlockSpec(memory_space=pltpu.HBM)

    def sems(*dims):
        return pltpu.SemaphoreType.DMA(dims)

    errors = (PAIRS, 2, LAYERS, TOKENS, TILE)
    staged, grad, squares = pl.pallas_call(
        exchange_kernel,
        name="exchange",
        out_shape=(
            pltpu.VMEM((2 * PAIRS, SLAB, LAYERS, TILE), bf16),
            jax.ShapeDtypeStruct((LAYERS, TOPK, TOKENS), f32),
            jax.ShapeDtypeStruct((8, TILE), f32),
        ),
        in_specs=[in_hbm] * 5,
        out_specs=(in_vmem, in_vmem, in_vmem),
        scratch_shapes=[
            pltpu.VMEM((2 * PAIRS, SLAB, LAYERS, TILE), bf16),
            pltpu.VMEM((TOPK, TOKENS), jnp.int32),
            pltpu.VMEM((TOPK, TOKENS), bf16),
            pltpu.VMEM((LAYERS, D), f32),
            pltpu.VMEM((TOKENS, LAYERS * SLAB), f32),
            pltpu.VMEM((LAYERS * TOKENS, LAYERS * SLAB), bf16),
            pltpu.VMEM((PAIRS, 2, LAYERS, HALF, TILE), f32),
            pltpu.VMEM((PAIRS, 2, LAYERS, HALF, TILE), bf16),
            pltpu.VMEM((PAIRS, 2, LAYERS, HALF, TILE), bf16),
            pltpu.VMEM((PAIRS, 2, LAYERS, HALF, TILE), bf16),
            pltpu.VMEM((2, 2, ROWS, TILE), bf16),
            pltpu.VMEM((2, 3, PAIRS, LAYERS, ROWS, TILE), bf16),
            pltpu.VMEM((2, PAIRS, LAYERS, ROWS, TILE), f32),
            pltpu.VMEM((2, PAIRS, LAYERS, ROWS, TILE), bf16),
            pltpu.VMEM((2, 3, PAIRS, ROWS, TILE), bf16),
            pltpu.VMEM((2, PAIRS, ROWS, TILE), f32),
            pltpu.VMEM((2, PAIRS, ROWS, TILE), bf16),
            pltpu.VMEM((2, 7, 2, ROWS, TILE), bf16),
            pltpu.VMEM(errors, bf16),
            pltpu.VMEM((SLAB, TOKENS), bf16),
            pltpu.VMEM((LAYERS * SLAB, LAYERS * TOKENS), bf16),
            pltpu.VMEM((8, TILE), f32),
            pltpu.VMEM((LAYERS, LAYERS * SLAB, TOKENS), f32),
            pltpu.VMEM((SLAB, TOKENS), f32),
            pltpu.VMEM((TOPK, TOKENS), f32),
            pltpu.VMEM((7, 8, TILE), f32),
            pltpu.VMEM((8, 2, 8, TILE), f32),
            pltpu.VMEM((2, 16, 2, 8, TILE), f32),
            sems(3), sems(2 * PAIRS), sems(2, 2),
            sems(GROUPS), sems(GROUPS), sems(2, GROUPS, 3), sems(2, GROUPS, 3),
            sems(2, GROUPS, 3), sems(2, GROUPS, 3), sems(2, 2, 7), sems(2, 2, 7),
            sems(2, 3), sems(2, 3), sems(2, GROUPS, 3), sems(2, GROUPS, 3),
            sems(GROUPS), sems(GROUPS), sems(2, 7), sems(2, 7),
            sems(7), sems(7), sems(7), sems(7), sems(15), sems(15), sems(1), sems(1),
        ],
        compiler_params=pltpu.CompilerParams(
            collective_id=0, has_side_effects=True, vmem_limit_bytes=40 << 20
        ),
    )(
        *[
            pltpu.with_memory_space_constraint(array, pltpu.HBM)
            for array in (
                decoder,
                jnp.transpose(code_index, (0, 2, 1)),
                jnp.transpose(code_value, (0, 2, 1)),
                bias,
                target,
            )
        ]
    )
    grads = pl.pallas_call(
        layout_kernel,
        name="decoder_gradient",
        out_shape=jax.ShapeDtypeStruct(decoder.shape, bf16),
        in_specs=[in_vmem],
        out_specs=in_hbm,
        scratch_shapes=[sems(2 * PAIRS)],
        compiler_params=pltpu.CompilerParams(vmem_limit_bytes=8 << 20),
    )(pltpu.with_memory_space_constraint(staged, pltpu.VMEM))
    layer_error = jnp.sum(squares[:LAYERS], axis=1) / (TOKENS * D)
    return layer_error, grads, jnp.transpose(grad, (0, 2, 1))


def solution(mesh):
    torus = Mesh(mesh.devices.reshape(2, 4, 2, 8, 2), AXES)
    rows = P(AXES, None, None)
    return jax.shard_map(
        on_device,
        mesh=torus,
        in_specs=(rows, P(), P(), P(), P()),
        out_specs=(P(), rows, P()),
        check_vma=False,
    )
```

time: 88.1 us -> 78 us (0.89)
  local copies, waits for them, and re-layouts: 7.16 us -> 0.66 us
  Pallas kernels: 79.3 us -> 76 us
    unnamed x11 -> x1, local copies, waits for them, and re-layouts: 7.16 us -> 0.66 us
    pallas_call x2, Pallas kernels: 79.3 us -> 76 us  [the longest x1 73.7 us: on_device(): pl.pallas_call(exchange_kernel, name='exchange', out_shape=(pltpu.VMEM((2...]
where the time goes in v2:
time: 78 us; the launch traced here: 77.9 us
  Pallas kernels  76 us (97%)
    pallas_call x1, Pallas kernels, on_device(): pl.pallas_call(exchange_kernel, name='exchange', out_shape=(pltpu.VMEM((2...  73.7 us
    pallas_call x1, Pallas kernels, on_device(): pl.pallas_call(layout_kernel, name='decoder_gradient', out_shape=jax.Shap...  2.31 us

profile of v2, /device:TPU:1, one launch (start us, length us, event | category | flops | bytes accessed | tf_op | source)
XLA Modules:
  0.0 77.9 jit_solution(12198454722217544323)
XLA Ops:
  0.6 73.7 %exchange.1 = (bf16[18,256,4,128]{3,2,1,0:T(4,128)(2,1)S(1)}, f32[4,64,128]{2,1,0:T(8,128)S(1)}, f32[8,128]{1,0:T(8,128)S(1)}) custom-call(bf16[256,4,2304]{2,1,0:T(4,128)(2,1)} %decoder.1, s32[4,64,128]{2,1,0:T(8,128)} %bitcast.4, bf16[4,64,128]{2,1,0:T(8,128)(2,1)} %bitcast.5, f32[4,2304]{1,0:T(4,128)} %bias_hbm.1, bf16[4,128,2304]{2,1,0:T(8,128)(2,1)} %target.1), custom_call_target="tpu_custom_call" | custom-call | tf_op jit(solution)/shard_map/exchange/pallas_call | solution.py:474
  74.3 0.1 slice_reduce_fusion
  74.4 0.5 broadcast_multiply_fusion
  74.9 2.3 %decoder_gradient.1 = bf16[256,4,2304]{2,1,0:T(4,128)(2,1)} custom-call(bf16[18,256,4,128]{3,2,1,0:T(4,128)(2,1)S(1)} %get-tuple-element.7.grads), custom_call_target="tpu_custom_call" | custom-call | tf_op jit(solution)/shard_map/decoder_gradient/pallas_call | solution.py:535
  77.2 0.7 copy.9

commit v3 on v2

--- a/solution.py
+++ b/solution.py
@@ -80,8 +80,8 @@
     decoder, index_hbm, value_hbm, bias_hbm, target,
     grads_out, grad_out, square_out,
     weights, index_ref, value_ref, bias_ref, spread_codes, forward, own, core_send, core_recv, own_b, target_v,
-    recv1, sum1, sum1_b, recv2, sum2, sum2_b, recv3,
-    error, codes, wide_codes, squares, products, sums, picked, pick_recv, by_z, by_plane,
+    recv1, sum1, sum1_b, recv2, sum2, send3, recv3,
+    error, by_z_error, codes, wide_codes, squares, products, sums, picked, pick_recv, by_z, by_plane,
     small_sem, weight_sem, target_sem,
     core_s, core_r, one_s, one_r, two_s, two_r, three_s, three_r,
     as_s, as_r, af_s, af_r, ac_s, ac_r,
@@ -113,31 +113,6 @@
             target_sem.at[p, which],
         )
 
-    barrier = pltpu.get_barrier_semaphore()
-
-    def z_peer(i):
-        return lax.rem(z + i, 8)
-
-    def at_plane(i):
-        return {"x": lax.rem(x + lax.rem(i, 4), 4), **at_y(lax.rem(y + i // 4, 4))}
-
-    def flip(position, by):
-        return position + by * (1 - 2 * lax.rem(position, 2))
-
-    def near(i):
-        return flip(x, lax.rem(i, 2)), flip(y, lax.rem(i // 2, 2)), flip(core, i // 4)
-
-    def at_near(i):
-        px, py, pc = near(i)
-        return {"x": px, "core": pc, **at_y(py)}
-
-    def greet(device):
-        pl.semaphore_signal(barrier, inc=1, device_id=device, device_id_type=MESH)
-
-    loop(1, 8, lambda i: greet(at_z(z_peer(i))))
-    loop(1, 16, lambda i: greet(at_plane(i)))
-    loop(4, 8, lambda i: greet(at_near(i)))
-
     small = [
         pltpu.make_async_copy(index_hbm.at[source], index_ref, small_sem.at[0]),
         pltpu.make_async_copy(value_hbm.at[source], value_ref, small_sem.at[1]),
@@ -151,6 +126,31 @@
         for which in range(2):
             target_copy(p, which).start()
 
+    barrier = pltpu.get_barrier_semaphore()
+
+    def z_peer(i):
+        return lax.rem(z + i, 8)
+
+    def at_plane(i):
+        return {"x": lax.rem(x + lax.rem(i, 4), 4), **at_y(lax.rem(y + i // 4, 4))}
+
+    def flip(position, by):
+        return position + by * (1 - 2 * lax.rem(position, 2))
+
+    def near(i):
+        return flip(x, lax.rem(i, 2)), flip(y, lax.rem(i // 2, 2)), flip(core, i // 4)
+
+    def at_near(i):
+        px, py, pc = near(i)
+        return {"x": px, "core": pc, **at_y(py)}
+
+    def greet(device):
+        pl.semaphore_signal(barrier, inc=1, device_id=device, device_id_type=MESH)
+
+    loop(1, 8, lambda i: greet(at_z(z_peer(i))))
+    loop(1, 16, lambda i: greet(at_plane(i)))
+    loop(4, 8, lambda i: greet(at_near(i)))
+
     for copy in small:
         copy.wait()
     latents = lax.broadcasted_iota(jnp.int32, (SLAB, TOKENS), 0)
@@ -196,16 +196,11 @@
             (two_s, two_r), (p, g, i - 1), at_second[p](k),
         )
 
-    def three_copy(p, which, i):
-        k = z_peer(i)
-        return remote(
-            sum2_b.at[p, k if which == 0 else PAIRS - 1], recv3.at[p, i - 1, which],
-            (three_s, three_r), (p, which, i - 1), at_z(k),
-        )
-
-    def z_copy(p, i):
-        tile = error.at[z, p, second[p], pl.ds(tokens_of[p], ROWS), :]
-        return remote(tile, tile, (az_s, az_r), (p, i - 1), at_z(z_peer(i)))
+    def three_copy(i):
+        return remote(send3.at[z_peer(i)], recv3.at[i - 1], (three_s, three_r), i - 1, at_z(z_peer(i)))
+
+    def z_copy(i):
+        return remote(by_z_error.at[z], by_z_error.at[z], (az_s, az_r), i - 1, at_z(z_peer(i)))
 
     def second_copy(p, i):
         tiles = error.at[:, p, second[p], pl.ds(tokens_of[p], ROWS), :]
@@ -260,54 +255,56 @@
         arrive(two_copy, g)
         for p in range(2):
 
-            def add(b):
+            for b in range(g * WIDE, (g + 1) * WIDE):
                 total = sum1[p, b, second[p]]
                 for k in range(3):
                     total = total + recv2[p, k, b].astype(f32)
                 sum2[p, b] = total
-                sum2_b[p, b] = total.astype(bf16)
-
-            loop(g * WIDE, (g + 1) * WIDE, add)
+                if b < 8:
+                    send3[b, 0, p] = total.astype(bf16)
+                else:
+                    for k in range(8):
+                        send3[k, 1, p] = total.astype(bf16)
 
     def add_z():
-        def send(i):
-            for p in range(2):
-                for which in range(2):
-                    three_copy(p, which, i).start()
-
-        loop(1, 8, send)
-        pending.extend(waits(1, 8, functools.partial(three_copy, p, which)) for p in range(2) for which in range(2))
+        loop(1, 8, lambda i: three_copy(i).start())
+        pending.append(waits(1, 8, three_copy))
 
     layer_row = lax.broadcasted_iota(jnp.int32, (LAYERS, TILE), 0)
     tile_row = lax.broadcasted_iota(jnp.int32, (8, TILE), 0)
 
     def take_errors():
         squared = jnp.zeros((8, TILE), f32)
+        loop(1, 8, lambda i: three_copy(i).wait_recv())
         for which in range(2):
             for p in range(2):
-                loop(1, 8, lambda i: three_copy(p, which, i).wait_recv())
                 target_copy(p, which).wait()
                 tile = z if which == 0 else PAIRS - 1
                 total = sum2[p, tile]
                 for i in range(7):
-                    total = total + recv3[p, i, which].astype(f32)
+                    total = total + recv3[i, which, p].astype(f32)
                 columns = pl.ds(pl.multiple_of((tile * 2 + p) * TILE, TILE), TILE)
                 shift = jnp.sum(jnp.where(layer_row == second[p], bias_ref[:, columns], 0.0), axis=0, keepdims=True)
                 residual = total + shift - target_v[p, which].astype(f32)
-                error[tile, p, second[p], pl.ds(tokens_of[p], ROWS), :] = residual.astype(bf16)
                 if which == 0:
-                    loop(1, 8, lambda i: z_copy(p, i).start())
-                    pending.append(waits(1, 8, functools.partial(z_copy, p)))
+                    by_z_error[z, p] = residual.astype(bf16)
+                else:
+                    error[tile, p, second[p], pl.ds(tokens_of[p], ROWS), :] = residual.astype(bf16)
                 square = jnp.sum(residual * residual, axis=0, keepdims=True)
                 counted = tile_row == second[p]
                 if which == 1:
                     counted = jnp.logical_and(counted, z == 0)
                 squared = squared + jnp.where(counted, square, 0.0)
+            if which == 0:
+                loop(1, 8, lambda i: z_copy(i).start())
+                pending.append(waits(1, 8, z_copy))
         squares[...] = squared
 
     def pass_layers():
+        loop(1, 8, lambda i: z_copy(i).wait_recv())
         for p in range(2):
-            loop(1, 8, lambda i: z_copy(p, i).wait_recv())
+            for b in range(8):
+                error[b, p, second[p], pl.ds(tokens_of[p], ROWS), :] = by_z_error[b, p]
             for i in range(1, 4):
                 second_copy(p, i).start()
                 pending.append(second_copy(p, i).wait_send)
@@ -335,10 +332,12 @@
     def project(g):
         for tile in range(2 * g * WIDE, 2 * (g + 1) * WIDE):
             weight_copy(tile).wait()
-        for b in range(g * WIDE, (g + 1) * WIDE):
-            product = contract(forward[...], jnp.concatenate([flat[2 * b], flat[2 * b + 1]], axis=1), 1, 0)
+        tiles = [flat[tile] for tile in range(2 * g * WIDE, 2 * (g + 1) * WIDE)]
+        product = contract(forward[...], jnp.concatenate(tiles, axis=1), 1, 0)
+        for i in range(WIDE):
+            b = g * WIDE + i
             for p in range(2):
-                columns = slice(p * TILE, (p + 1) * TILE)
+                columns = slice((2 * i + p) * TILE, (2 * i + p + 1) * TILE)
                 own[b, p] = product[: LAYERS * HALF, columns].reshape(LAYERS, HALF, TILE)
                 core_send[b, p] = product[LAYERS * HALF :, columns].reshape(LAYERS, HALF, TILE).astype(bf16)
 
@@ -392,11 +391,11 @@
     flat_out = grads_out.reshape(2 * PAIRS, LAYERS * SLAB, TILE)
 
     def decoder_gradients(g):
-        for b in range(g * WIDE, (g + 1) * WIDE):
-            both = [error[b, p].reshape(LAYERS * TOKENS, TILE) for p in range(2)]
-            product = contract(wide_codes[...], jnp.concatenate(both, axis=1), 1, 0).astype(bf16)
-            for p in range(2):
-                flat_out[2 * b + p] = product[:, p * TILE : (p + 1) * TILE]
+        tiles = range(2 * g * WIDE, 2 * (g + 1) * WIDE)
+        errors = [error[tile // 2, tile % 2].reshape(LAYERS * TOKENS, TILE) for tile in tiles]
+        product = contract(wide_codes[...], jnp.concatenate(errors, axis=1), 1, 0).astype(bf16)
+        for i, tile in enumerate(tiles):
+            flat_out[tile] = product[:, i * TILE : (i + 1) * TILE]
 
     def rank(px, py, pc):
         return lax.rem(px, 2) + 2 * lax.rem(py, 2) + 4 * pc
@@ -452,13 +451,16 @@
     pending[-1]()
 
 
-def layout_kernel(grads, out, sems):
+def write_kernel(staged, grad, squares, grads, grad_out, error_out, sems):
     copies = [
-        pltpu.make_async_copy(grads.at[tile], out.at[:, :, pl.ds(tile * TILE, TILE)], sems.at[tile])
+        pltpu.make_async_copy(staged.at[tile], grads.at[:, :, pl.ds(tile * TILE, TILE)], sems.at[tile])
         for tile in range(2 * PAIRS)
     ]
+    copies.append(pltpu.make_async_copy(grad, grad_out, sems.at[2 * PAIRS]))
     for copy in copies:
         copy.start()
+    for t in range(LAYERS):
+        error_out[t] = jnp.sum(squares[t : t + 1, :]) * (1.0 / (TOKENS * D))
     for copy in copies:
         copy.wait()
 
@@ -498,9 +500,10 @@
             pltpu.VMEM((2, PAIRS, LAYERS, ROWS, TILE), bf16),
             pltpu.VMEM((2, 3, PAIRS, ROWS, TILE), bf16),
             pltpu.VMEM((2, PAIRS, ROWS, TILE), f32),
-            pltpu.VMEM((2, PAIRS, ROWS, TILE), bf16),
-            pltpu.VMEM((2, 7, 2, ROWS, TILE), bf16),
+            pltpu.VMEM((8, 2, 2, ROWS, TILE), bf16),
+            pltpu.VMEM((7, 2, 2, ROWS, TILE), bf16),
             pltpu.VMEM(errors, bf16),
+            pltpu.VMEM((8, 2, ROWS, TILE), bf16),
             pltpu.VMEM((SLAB, TOKENS), bf16),
             pltpu.VMEM((LAYERS * SLAB, LAYERS * TOKENS), bf16),
             pltpu.VMEM((8, TILE), f32),
@@ -512,9 +515,9 @@
             pltpu.VMEM((2, 16, 2, 8, TILE), f32),
             sems(3), sems(2 * PAIRS), sems(2, 2),
             sems(GROUPS), sems(GROUPS), sems(2, GROUPS, 3), sems(2, GROUPS, 3),
-            sems(2, GROUPS, 3), sems(2, GROUPS, 3), sems(2, 2, 7), sems(2, 2, 7),
+            sems(2, GROUPS, 3), sems(2, GROUPS, 3), sems(7), sems(7),
             sems(2, 3), sems(2, 3), sems(2, GROUPS, 3), sems(2, GROUPS, 3),
-            sems(GROUPS), sems(GROUPS), sems(2, 7), sems(2, 7),
+            sems(GROUPS), sems(GROUPS), sems(7), sems(7),
             sems(7), sems(7), sems(7), sems(7), sems(15), sems(15), sems(1), sems(1),
         ],
         compiler_params=pltpu.CompilerParams(
@@ -532,17 +535,20 @@
             )
         ]
     )
-    grads = pl.pallas_call(
-        layout_kernel,
-        name="decoder_gradient",
-        out_shape=jax.ShapeDtypeStruct(decoder.shape, bf16),
-        in_specs=[in_vmem],
-        out_specs=in_hbm,
-        scratch_shapes=[sems(2 * PAIRS)],
+    grads, code_grad, layer_error = pl.pallas_call(
+        write_kernel,
+        name="write_outputs",
+        out_shape=(
+            jax.ShapeDtypeStruct(decoder.shape, bf16),
+            jax.ShapeDtypeStruct((LAYERS, TOPK, TOKENS), f32),
+            jax.ShapeDtypeStruct((LAYERS,), f32),
+        ),
+        in_specs=[in_vmem] * 3,
+        out_specs=(in_hbm, in_hbm, pl.BlockSpec(memory_space=pltpu.SMEM)),
+        scratch_shapes=[sems(2 * PAIRS + 1)],
         compiler_params=pltpu.CompilerParams(vmem_limit_bytes=8 << 20),
-    )(pltpu.with_memory_space_constraint(staged, pltpu.VMEM))
-    layer_error = jnp.sum(squares[:LAYERS], axis=1) / (TOKENS * D)
-    return layer_error, grads, jnp.transpose(grad, (0, 2, 1))
+    )(*[pltpu.with_memory_space_constraint(array, pltpu.VMEM) for array in (staged, grad, squares)])
+    return layer_error, grads, jnp.transpose(code_grad, (0, 2, 1))
 
 
 def solution(mesh):

time: 78 us -> 76.6 us (0.982)
  no operation moved by 1% of the time
where the time goes in v3:
time: 76.6 us; the launch traced here: 76.5 us
  Pallas kernels  75.8 us (99%)
    pallas_call x1, Pallas kernels, on_device(): pl.pallas_call(exchange_kernel, name='exchange', out_shape=(pltpu.VMEM((2...  73 us
    pallas_call x1, Pallas kernels, on_device(): pl.pallas_call(write_kernel, name='write_outputs', out_shape=(jax.ShapeDt...  2.87 us

profile of v3, /device:TPU:1, one launch (start us, length us, event | category | flops | bytes accessed | tf_op | source)
XLA Modules:
  0.0 76.5 jit_solution(8714856968180702267)
XLA Ops:
  0.6 73.0 %exchange.1 = (bf16[18,256,4,128]{3,2,1,0:T(4,128)(2,1)S(1)}, f32[4,64,128]{2,1,0:T(8,128)S(1)}, f32[8,128]{1,0:T(8,128)S(1)}) custom-call(bf16[256,4,2304]{2,1,0:T(4,128)(2,1)} %decoder.1, s32[4,64,128]{2,1,0:T(8,128)} %bitcast.3, bf16[4,64,128]{2,1,0:T(8,128)(2,1)} %bitcast.4, f32[4,2304]{1,0:T(4,128)} %bias_hbm.1, bf16[4,128,2304]{2,1,0:T(8,128)(2,1)} %target.1), custom_call_target="tpu_custom_call" | custom-call | tf_op jit(solution)/shard_map/exchange/pallas_call | solution.py:476
  73.6 2.9 %write_outputs.1 = (bf16[256,4,2304]{2,1,0:T(4,128)(2,1)}, f32[4,64,128]{2,1,0:T(8,128)}, f32[4]{0:T(128)}) custom-call(bf16[18,256,4,128]{3,2,1,0:T(4,128)(2,1)S(1)} %get-tuple-element.9.staged, f32[4,64,128]{2,1,0:T(8,128)S(1)} %get-tuple-element.10.grad, f32[8,128]{1,0:T(8,128)S(1)} %get-tuple-element.11.squares), custom_call_target="tpu_custom_call" | custom-call | tf_op jit(solution)/shard_map/write_outputs/pallas_call | solution.py:538

commit v4 on v3

--- a/solution.py
+++ b/solution.py
@@ -126,6 +126,10 @@
         for which in range(2):
             target_copy(p, which).start()
 
+    for b in range(PAIRS):
+        for p in range(2):
+            error[b, p, 0] = jnp.zeros((TOKENS, TILE), bf16)
+
     barrier = pltpu.get_barrier_semaphore()
 
     def z_peer(i):
@@ -181,11 +185,14 @@
     def core_copy(g):
         return remote(core_send.at[group(g)], core_recv.at[group(g)], (core_s, core_r), g, other)
 
-    def one_copy(g, p, i):
+    def layers(low):
+        return pl.ds(low, LAYERS - low)
+
+    def one_copy(low, g, p, i):
         k = lax.rem(first[p] + i, 4)
         rows = pl.ds(pl.multiple_of(k * ROWS, ROWS), ROWS)
         return remote(
-            own_b.at[group(g), p, :, rows, :], recv1.at[p, i - 1, group(g)],
+            own_b.at[group(g), p, layers(low), rows, :], recv1.at[p, i - 1, group(g), layers(low)],
             (one_s, one_r), (p, g, i - 1), at_first[p](k),
         )
 
@@ -206,13 +213,42 @@
         tiles = error.at[:, p, second[p], pl.ds(tokens_of[p], ROWS), :]
         return remote(tiles, tiles, (as_s, as_r), (p, i - 1), at_second[p](lax.rem(second[p] + i, 4)))
 
-    def first_copy(g, p, i):
-        tiles = error.at[group(g), p, :, pl.ds(tokens_of[p], ROWS), :]
+    def first_copy(low, g, p, i):
+        tiles = error.at[group(g), p, layers(low), pl.ds(tokens_of[p], ROWS), :]
         return remote(tiles, tiles, (af_s, af_r), (p, g, i - 1), at_first[p](lax.rem(first[p] + i, 4)))
 
     def half_copy(g):
         tiles = error.at[group(g), :, :, pl.ds(pl.multiple_of(core * HALF, HALF), HALF), :]
         return remote(tiles, tiles, (ac_s, ac_r), g, other)
+
+    def no_source(p, position):
+        across = lax.axis_index("yh") if p == 0 else lax.axis_index("x") // 2
+        return jnp.logical_or(across > 0, position > 1)
+
+    def either(late, do):
+        @pl.when(late)
+        def _():
+            do(1)
+
+        @pl.when(jnp.logical_not(late))
+        def _():
+            do(0)
+
+    def one_start(g, p, i):
+        either(source > 0, lambda low: one_copy(low, g, p, i).start())
+        pending.append(lambda: either(source > 0, lambda low: one_copy(low, g, p, i).wait_send()))
+
+    def one_arrive(g, p, i):
+        late = no_source(p, lax.rem(first[p] + 4 - i, 4))
+        either(late, lambda low: one_copy(low, g, p, i).wait_recv())
+
+    def first_start(g, p, i):
+        late = no_source(p, lax.rem(first[p] + i, 4))
+        either(late, lambda low: first_copy(low, g, p, i).start())
+        pending.append(lambda: either(late, lambda low: first_copy(low, g, p, i).wait_send()))
+
+    def first_arrive(g, p, i):
+        either(source > 0, lambda low: first_copy(low, g, p, i).wait_recv())
 
     def exchange(copy, g):
         for i in range(1, 4):
@@ -225,6 +261,8 @@
             for i in range(1, 4):
                 copy(g, p, i).wait_recv()
 
+    layer_of = lax.broadcasted_iota(jnp.int32, (LAYERS, ROWS, TILE), 0)
+
     def add_core(g):
         core_copy(g).wait_recv()
 
@@ -235,16 +273,22 @@
             own_b[b, p] = total.astype(bf16)
 
         loop(0, 2 * WIDE, add)
-        exchange(one_copy, g)
+        for i in range(1, 4):
+            for p in range(2):
+                one_start(g, p, i)
 
     def add_first(g):
-        arrive(one_copy, g)
+        for p in range(2):
+            for i in range(1, 4):
+                one_arrive(g, p, i)
         for p in range(2):
 
             def add(b):
                 total = own[b, p, :, pl.ds(pl.multiple_of(first[p] * ROWS, ROWS), ROWS), :]
                 for i in range(3):
-                    total = total + recv1[p, i, b].astype(f32)
+                    part = recv1[p, i, b].astype(f32)
+                    late = no_source(p, lax.rem(first[p] + 3 - i, 4))
+                    total = total + jnp.where(jnp.logical_and(late, layer_of == 0), 0.0, part)
                 sum1[p, b] = total
                 sum1_b[p, b] = total.astype(bf16)
 
@@ -313,7 +357,9 @@
                 second_copy(p, i).wait_recv()
 
     def pass_rows(g):
-        arrive(first_copy, g)
+        for p in range(2):
+            for i in range(1, 4):
+                first_arrive(g, p, i)
         half_copy(g).start()
         pending.append(half_copy(g).wait_send)
 
@@ -367,7 +413,9 @@
     take_errors()
     pass_layers()
     for g in range(GROUPS):
-        exchange(first_copy, g)
+        for i in range(1, 4):
+            for p in range(2):
+                first_start(g, p, i)
     for g in range(GROUPS):
         pass_rows(g)
         if g > 0:

time: 76.6 us -> 74.8 us (0.977)
  Pallas kernels: 75.8 us -> 74.1 us
    pallas_call x1, Pallas kernels: 73 us -> 71.2 us  [on_device(): pl.pallas_call(exchange_kernel, name='exchange', out_shape=(pltpu.VMEM((2...]
where the time goes in v4:
time: 74.8 us; the launch traced here: 74.7 us
  Pallas kernels  74.1 us (99%)
    pallas_call x1, Pallas kernels, on_device(): pl.pallas_call(exchange_kernel, name='exchange', out_shape=(pltpu.VMEM((2...  71.2 us
    pallas_call x1, Pallas kernels, on_device(): pl.pallas_call(write_kernel, name='write_outputs', out_shape=(jax.ShapeDt...  2.87 us

profile of v4, /device:TPU:1, one launch (start us, length us, event | category | flops | bytes accessed | tf_op | source)
XLA Modules:
  0.0 74.7 jit_solution(8112730218180664599)
XLA Ops:
  0.6 71.2 %exchange.1 = (bf16[18,256,4,128]{3,2,1,0:T(4,128)(2,1)S(1)}, f32[4,64,128]{2,1,0:T(8,128)S(1)}, f32[8,128]{1,0:T(8,128)S(1)}) custom-call(bf16[256,4,2304]{2,1,0:T(4,128)(2,1)} %decoder.1, s32[4,64,128]{2,1,0:T(8,128)} %bitcast.3, bf16[4,64,128]{2,1,0:T(8,128)(2,1)} %bitcast.4, f32[4,2304]{1,0:T(4,128)} %bias_hbm.1, bf16[4,128,2304]{2,1,0:T(8,128)(2,1)} %target.1), custom_call_target="tpu_custom_call" | custom-call | tf_op jit(solution)/shard_map/exchange/pallas_call | solution.py:524
  71.8 2.9 %write_outputs.1 = (bf16[256,4,2304]{2,1,0:T(4,128)(2,1)}, f32[4,64,128]{2,1,0:T(8,128)}, f32[4]{0:T(128)}) custom-call(bf16[18,256,4,128]{3,2,1,0:T(4,128)(2,1)S(1)} %get-tuple-element.9.staged, f32[4,64,128]{2,1,0:T(8,128)S(1)} %get-tuple-element.10.grad, f32[8,128]{1,0:T(8,128)S(1)} %get-tuple-element.11.squares), custom_call_target="tpu_custom_call" | custom-call | tf_op jit(solution)/shard_map/write_outputs/pallas_call | solution.py:586
